TPU v7x, 32 devices: a whole 2x2x4 slice. The times are simulated.
32 devices in a mesh: seq: 2 (over y), ctx: 4 (over x, core), wt: 4 (over z).
Axes of the slice: x: 2, y: 2, z: 4, core: 2. Of those that a mesh axis runs over, the one named last changes fastest.
Arguments:
- tokens: bfloat16 [16, 1024, 768], P(('seq', 'wt'), 'ctx'), may hold values from -6 to 6
- cotangent: bfloat16 [16, 1024, 768], P(('seq', 'wt'), 'ctx'), may hold values from -6 to 6
- segment_ids: int32 [16, 1024], P(('seq', 'wt'), 'ctx'), may hold values from 0 to 4, as said below
- lengths: int32 [16, 4], P(('seq', 'wt')), may hold values from 32 to 928, as said below
- w_query: bfloat16 [768, 768], P('wt'), may hold values from -0.21875 to 0.21875
- b_query: bfloat16 [768], P('wt'), may hold values from -3 to 3
- w_key: bfloat16 [768, 768], P('wt'), may hold values from -0.21875 to 0.21875
- w_value: bfloat16 [768, 768], P('wt'), may hold values from -0.21875 to 0.21875
- b_value: bfloat16 [768], P('wt'), may hold values from -3 to 3
- w_attn: bfloat16 [768, 768], P('wt'), may hold values from -1.75 to 1.75
- b_attn: bfloat16 [768], P('wt'), may hold values from -2 to 2
- ln1_gain: bfloat16 [768], P('wt'), may hold values from 0.5 to 1.5
- ln1_shift: bfloat16 [768], P('wt'), may hold values from -2 to 2
- w_inner: bfloat16 [768, 3072], P('wt'), may hold values from -0.21875 to 0.21875
- b_inner: bfloat16 [3072], P('wt'), may hold values from -3 to 3
- w_outer: bfloat16 [3072, 768], P('wt'), may hold values from -0.109375 to 0.109375
- b_outer: bfloat16 [768], P('wt'), may hold values from -2 to 2
- ln2_gain: bfloat16 [768], P('wt'), may hold values from 0.5 to 1.5
- ln2_shift: bfloat16 [768], P('wt'), may hold values from -2 to 2
Outputs:
- layer_out: bfloat16 [16, 1024, 768], P(('seq', 'wt'), 'ctx')
- grad_input: bfloat16 [16, 1024, 768], P(('seq', 'wt'), 'ctx')
- grad_w_query: float32 [768, 768], P('wt')
- grad_b_query: float32 [768], P('wt')
- grad_w_key: float32 [768, 768], P('wt')
- grad_w_value: float32 [768, 768], P('wt')
- grad_b_value: float32 [768], P('wt')
- grad_w_attn: float32 [768, 768], P('wt')
- grad_b_attn: float32 [768], P('wt')
- grad_ln1_gain: float32 [768], P('wt')
- grad_ln1_shift: float32 [768], P('wt')
- grad_w_inner: float32 [768, 3072], P('wt')
- grad_b_inner: float32 [3072], P('wt')
- grad_w_outer: float32 [3072, 768], P('wt')
- grad_b_outer: float32 [768], P('wt')
- grad_ln2_gain: float32 [768], P('wt')
- grad_ln2_shift: float32 [768], P('wt')
Inputs may be any that keep to these rules, and one draw needn't show every extreme that they name: `lengths`: the 4 documents of a sequence lie end to end from its first position, and the positions after them are padding; among the 2 sequences that one device holds, one has a single document of 1024 - 3 * max(1, 32) positions, at a place among its documents that varies, and its other documents have max(1, 32) positions each; every other sequence has documents of 64 to 256 positions. `segment_ids`: position t holds d + 1 where it lies in the sequence's document d (counted from 0 in the order of lengths), and 0 in the padding.
All inputs are finite; a program needn't handle non-finite values.
Results may differ from a plain program's by a relative error of at most 0.02.
Values may be sent and summed in bfloat16 or wider, within the bound.
No kernel may reach another device: no remote copies, remote signals or barrier semaphores. Data moves between devices by JAX's collectives and lax.ppermute only.
A program may use at most 320 MiB of HBM per device.

v0:
```python
import math
import jax
import jax.numpy as jnp
from jax import lax
from jax.sharding import PartitionSpec as P

H = 12
HD = 64
NEG = -1000000000.0
EPS = 1e-05


def product(former, latter):
    return jnp.dot(former, latter, preferred_element_type=jnp.float32)


def over_rows(former, latter):
    return lax.dot_general(
        former, latter, (((0,), (0,)), ((), ())), preferred_element_type=jnp.float32
    )


def against(former, latter):
    return lax.dot_general(
        former, latter, (((1,), (1,)), ((), ())), preferred_element_type=jnp.float32
    )


def norm_rows(values, gain, shift):
    center = jnp.mean(values, axis=-1, keepdims=True)
    offset = values - center
    spread = jnp.mean(offset * offset, axis=-1, keepdims=True)
    return offset * lax.rsqrt(spread + EPS) * gain + shift


def exact_gelu(values):
    return jax.nn.gelu(values, approximate=False)


def key_segments(doc_lens, length):
    doc_ends = jnp.cumsum(doc_lens, axis=-1)
    places = jnp.arange(length, dtype=jnp.int32)
    passed = jnp.sum((places[None, :, None] >= doc_ends[:, None, :]).astype(jnp.int32), axis=-1)
    return jnp.where(places[None, :] < doc_ends[:, -1:], passed + 1, 0)


def to_items(matrix, groups):
    seq_count, length, model_width = matrix.shape
    per_group = model_width // (groups * HD)
    shaped = matrix.reshape(seq_count, length, groups, per_group, HD)
    return shaped.transpose(0, 2, 3, 1, 4).reshape(seq_count * groups, per_group, length, HD)


def from_items(blocks, seq_count):
    count_items, per_group, length, head_size = blocks.shape
    groups = count_items // seq_count
    shaped = blocks.reshape(seq_count, groups, per_group, length, head_size)
    return shaped.transpose(0, 3, 1, 2, 4).reshape(
        seq_count, length, groups * per_group * head_size
    )


def masked_scores(head_q, head_k, q_seg, k_seg, factor):
    scores = jnp.einsum("hqd,hkd->hqk", head_q, head_k, preferred_element_type=jnp.float32) * factor
    matching = q_seg[:, None] == k_seg[None, :]
    return jnp.where(matching[None], scores, NEG)


def body(
    tokens,
    cotangent,
    segment_ids,
    lengths,
    w_query,
    b_query,
    w_key,
    w_value,
    b_value,
    w_attn,
    b_attn,
    ln1_gain,
    ln1_shift,
    w_inner,
    b_inner,
    w_outer,
    b_outer,
    ln2_gain,
    ln2_shift,
):
    shards = (
        w_query,
        b_query,
        w_key,
        w_value,
        b_value,
        w_attn,
        b_attn,
        ln1_gain,
        ln1_shift,
        w_inner,
        b_inner,
        w_outer,
        b_outer,
        ln2_gain,
        ln2_shift,
    )
    seq_count, shard_len, model_width = tokens.shape
    row_count = seq_count * shard_len
    groups = H // math.gcd(H, 4)
    factor = 1.0 / math.sqrt(HD)
    full = (
        lax.all_gather(shards[0], "wt", axis=0, tiled=True),
        lax.all_gather(shards[1], "wt", axis=0, tiled=True),
        lax.all_gather(shards[2], "wt", axis=0, tiled=True),
        lax.all_gather(shards[3], "wt", axis=0, tiled=True),
        lax.all_gather(shards[4], "wt", axis=0, tiled=True),
        lax.all_gather(shards[5], "wt", axis=0, tiled=True),
        lax.all_gather(shards[6], "wt", axis=0, tiled=True),
        lax.all_gather(shards[7], "wt", axis=0, tiled=True),
        lax.all_gather(shards[8], "wt", axis=0, tiled=True),
        lax.all_gather(shards[9], "wt", axis=0, tiled=True),
        lax.all_gather(shards[10], "wt", axis=0, tiled=True),
        lax.all_gather(shards[11], "wt", axis=0, tiled=True),
        lax.all_gather(shards[12], "wt", axis=0, tiled=True),
        lax.all_gather(shards[13], "wt", axis=0, tiled=True),
        lax.all_gather(shards[14], "wt", axis=0, tiled=True),
    )
    rows = tokens.reshape(row_count, model_width)
    query = (product(rows, full[0]) + full[1].astype(jnp.float32)).astype(jnp.bfloat16)
    key_rows = product(rows, full[2]).astype(jnp.bfloat16)
    value_rows = (product(rows, full[3]) + full[4].astype(jnp.float32)).astype(jnp.bfloat16)
    local_kv = (
        key_rows.reshape(seq_count, shard_len, model_width),
        value_rows.reshape(seq_count, shard_len, model_width),
    )
    whole_kv = (
        lax.all_gather(local_kv[0], "ctx", axis=1, tiled=True),
        lax.all_gather(local_kv[1], "ctx", axis=1, tiled=True),
    )
    seq_len = whole_kv[0].shape[1]
    key_segs = jnp.repeat(key_segments(lengths, seq_len), groups, axis=0)
    query_segs = jnp.repeat(segment_ids, groups, axis=0)
    query_items = to_items(query.reshape(seq_count, shard_len, model_width), groups)
    key_items = to_items(whole_kv[0], groups)
    value_items = to_items(whole_kv[1], groups)

    def attend(item):
        head_q, head_k, head_v, q_seg, k_seg = item
        scores = masked_scores(head_q, head_k, q_seg, k_seg, factor)
        highest = jnp.max(scores, axis=-1, keepdims=True)
        totals = jnp.sum(jnp.exp(scores - highest), axis=-1, keepdims=True)
        log_sum = highest + jnp.log(totals)
        probs = jnp.exp(scores - log_sum).astype(jnp.bfloat16)
        mixed = jnp.einsum("hqk,hkd->hqd", probs, head_v, preferred_element_type=jnp.float32)
        return (mixed, log_sum[..., 0])

    attn_items, log_sums = lax.map(
        attend, (query_items, key_items, value_items, query_segs, key_segs)
    )
    attn = from_items(attn_items, seq_count).reshape(row_count, model_width).astype(jnp.bfloat16)
    first_sum = rows.astype(jnp.float32) + product(attn, full[5]) + full[6].astype(jnp.float32)
    hidden, first_pull = jax.vjp(
        norm_rows, first_sum, full[7].astype(jnp.float32), full[8].astype(jnp.float32)
    )
    hidden_low = hidden.astype(jnp.bfloat16)
    inner = product(hidden_low, full[9]) + full[10].astype(jnp.float32)
    active, gelu_pull = jax.vjp(exact_gelu, inner)
    active_low = active.astype(jnp.bfloat16)
    second_sum = hidden + product(active_low, full[11]) + full[12].astype(jnp.float32)
    result, second_pull = jax.vjp(
        norm_rows, second_sum, full[13].astype(jnp.float32), full[14].astype(jnp.float32)
    )
    layer_out = result.astype(jnp.bfloat16).reshape(tokens.shape)
    back = (
        lax.all_gather(shards[0], "wt", axis=0, tiled=True),
        lax.all_gather(shards[1], "wt", axis=0, tiled=True),
        lax.all_gather(shards[2], "wt", axis=0, tiled=True),
        lax.all_gather(shards[3], "wt", axis=0, tiled=True),
        lax.all_gather(shards[4], "wt", axis=0, tiled=True),
        lax.all_gather(shards[5], "wt", axis=0, tiled=True),
        lax.all_gather(shards[6], "wt", axis=0, tiled=True),
        lax.all_gather(shards[7], "wt", axis=0, tiled=True),
        lax.all_gather(shards[8], "wt", axis=0, tiled=True),
        lax.all_gather(shards[9], "wt", axis=0, tiled=True),
        lax.all_gather(shards[10], "wt", axis=0, tiled=True),
        lax.all_gather(shards[11], "wt", axis=0, tiled=True),
        lax.all_gather(shards[12], "wt", axis=0, tiled=True),
        lax.all_gather(shards[13], "wt", axis=0, tiled=True),
        lax.all_gather(shards[14], "wt", axis=0, tiled=True),
    )
    back_kv = (
        lax.all_gather(local_kv[0], "ctx", axis=1, tiled=True),
        lax.all_gather(local_kv[1], "ctx", axis=1, tiled=True),
    )
    back_keys = to_items(back_kv[0], groups)
    back_values = to_items(back_kv[1], groups)
    live = (segment_ids != 0).astype(jnp.float32).reshape(row_count, 1)
    grad_rows = cotangent.reshape(row_count, model_width).astype(jnp.float32) * live
    d_second, d_gain_two, d_shift_two = second_pull(grad_rows)
    d_outer = d_second.astype(jnp.bfloat16)
    g_w_outer = over_rows(active_low, d_outer)
    g_b_outer = jnp.sum(d_outer.astype(jnp.float32), axis=0)
    d_inner = gelu_pull(against(d_outer, back[11]))[0].astype(jnp.bfloat16)
    g_w_inner = over_rows(hidden_low, d_inner)
    g_b_inner = jnp.sum(d_inner.astype(jnp.float32), axis=0)
    d_hidden = d_second + against(d_inner, back[9])
    d_first, d_gain_one, d_shift_one = first_pull(d_hidden)
    d_proj = d_first.astype(jnp.bfloat16)
    g_w_attn = over_rows(attn, d_proj)
    g_b_attn = jnp.sum(d_proj.astype(jnp.float32), axis=0)
    d_attn = against(d_proj, back[5]).astype(jnp.bfloat16)
    d_attn_seq = d_attn.reshape(seq_count, shard_len, model_width)
    d_items = to_items(d_attn_seq, groups)

    def attend_back(item):
        head_q, head_k, head_v, q_seg, k_seg, log_sum, head_d = item
        scores = masked_scores(head_q, head_k, q_seg, k_seg, factor)
        probs = jnp.exp(scores - log_sum[..., None])
        d_probs = jnp.einsum("hqd,hkd->hqk", head_d, head_v, preferred_element_type=jnp.float32)
        center = jnp.sum(probs * d_probs, axis=-1, keepdims=True)
        d_scores = (probs * (d_probs - center)).astype(jnp.bfloat16)
        d_vals = jnp.einsum(
            "hqk,hqd->hkd", probs.astype(jnp.bfloat16), head_d, preferred_element_type=jnp.float32
        )
        d_q = (
            jnp.einsum("hqk,hkd->hqd", d_scores, head_k, preferred_element_type=jnp.float32)
            * factor
        )
        d_k = (
            jnp.einsum("hqk,hqd->hkd", d_scores, head_q, preferred_element_type=jnp.float32)
            * factor
        )
        return (d_q, d_k, d_vals)

    dq_items, dk_items, dv_items = lax.map(
        attend_back, (query_items, back_keys, back_values, query_segs, key_segs, log_sums, d_items)
    )
    d_query = from_items(dq_items, seq_count).reshape(row_count, model_width).astype(jnp.bfloat16)
    partial_kv = (from_items(dk_items, seq_count), from_items(dv_items, seq_count))
    own_kv = (
        lax.psum_scatter(
            partial_kv[0].astype(jnp.bfloat16), "ctx", scatter_dimension=1, tiled=True
        ).astype(jnp.float32),
        lax.psum_scatter(
            partial_kv[1].astype(jnp.bfloat16), "ctx", scatter_dimension=1, tiled=True
        ).astype(jnp.float32),
    )
    d_key = own_kv[0].reshape(row_count, model_width).astype(jnp.bfloat16)
    d_value = own_kv[1].reshape(row_count, model_width).astype(jnp.bfloat16)
    g_w_query = over_rows(rows, d_query)
    g_b_query = jnp.sum(d_query.astype(jnp.float32), axis=0)
    g_w_key = over_rows(rows, d_key)
    g_w_value = over_rows(rows, d_value)
    g_b_value = jnp.sum(d_value.astype(jnp.float32), axis=0)
    input_sum = (
        d_first + against(d_query, back[0]) + against(d_key, back[2]) + against(d_value, back[3])
    )
    grad_input = input_sum.astype(jnp.bfloat16).reshape(tokens.shape)
    grads = (
        g_w_query,
        g_b_query,
        g_w_key,
        g_w_value,
        g_b_value,
        g_w_attn,
        g_b_attn,
        d_gain_one,
        d_shift_one,
        g_w_inner,
        g_b_inner,
        g_w_outer,
        g_b_outer,
        d_gain_two,
        d_shift_two,
    )
    shares = (
        lax.psum_scatter(
            grads[0].astype(jnp.bfloat16), "wt", scatter_dimension=0, tiled=True
        ).astype(jnp.float32),
        lax.psum_scatter(
            grads[1].astype(jnp.bfloat16), "wt", scatter_dimension=0, tiled=True
        ).astype(jnp.float32),
        lax.psum_scatter(
            grads[2].astype(jnp.bfloat16), "wt", scatter_dimension=0, tiled=True
        ).astype(jnp.float32),
        lax.psum_scatter(
            grads[3].astype(jnp.bfloat16), "wt", scatter_dimension=0, tiled=True
        ).astype(jnp.float32),
        lax.psum_scatter(
            grads[4].astype(jnp.bfloat16), "wt", scatter_dimension=0, tiled=True
        ).astype(jnp.float32),
        lax.psum_scatter(
            grads[5].astype(jnp.bfloat16), "wt", scatter_dimension=0, tiled=True
        ).astype(jnp.float32),
        lax.psum_scatter(
            grads[6].astype(jnp.bfloat16), "wt", scatter_dimension=0, tiled=True
        ).astype(jnp.float32),
        lax.psum_scatter(
            grads[7].astype(jnp.bfloat16), "wt", scatter_dimension=0, tiled=True
        ).astype(jnp.float32),
        lax.psum_scatter(
            grads[8].astype(jnp.bfloat16), "wt", scatter_dimension=0, tiled=True
        ).astype(jnp.float32),
        lax.psum_scatter(
            grads[9].astype(jnp.bfloat16), "wt", scatter_dimension=0, tiled=True
        ).astype(jnp.float32),
        lax.psum_scatter(
            grads[10].astype(jnp.bfloat16), "wt", scatter_dimension=0, tiled=True
        ).astype(jnp.float32),
        lax.psum_scatter(
            grads[11].astype(jnp.bfloat16), "wt", scatter_dimension=0, tiled=True
        ).astype(jnp.float32),
        lax.psum_scatter(
            grads[12].astype(jnp.bfloat16), "wt", scatter_dimension=0, tiled=True
        ).astype(jnp.float32),
        lax.psum_scatter(
            grads[13].astype(jnp.bfloat16), "wt", scatter_dimension=0, tiled=True
        ).astype(jnp.float32),
        lax.psum_scatter(
            grads[14].astype(jnp.bfloat16), "wt", scatter_dimension=0, tiled=True
        ).astype(jnp.float32),
    )
    summed = (
        lax.psum(shares[0].astype(jnp.bfloat16), ("seq", "ctx")).astype(jnp.float32),
        lax.psum(shares[1].astype(jnp.bfloat16), ("seq", "ctx")).astype(jnp.float32),
        lax.psum(shares[2].astype(jnp.bfloat16), ("seq", "ctx")).astype(jnp.float32),
        lax.psum(shares[3].astype(jnp.bfloat16), ("seq", "ctx")).astype(jnp.float32),
        lax.psum(shares[4].astype(jnp.bfloat16), ("seq", "ctx")).astype(jnp.float32),
        lax.psum(shares[5].astype(jnp.bfloat16), ("seq", "ctx")).astype(jnp.float32),
        lax.psum(shares[6].astype(jnp.bfloat16), ("seq", "ctx")).astype(jnp.float32),
        lax.psum(shares[7].astype(jnp.bfloat16), ("seq", "ctx")).astype(jnp.float32),
        lax.psum(shares[8].astype(jnp.bfloat16), ("seq", "ctx")).astype(jnp.float32),
        lax.psum(shares[9].astype(jnp.bfloat16), ("seq", "ctx")).astype(jnp.float32),
        lax.psum(shares[10].astype(jnp.bfloat16), ("seq", "ctx")).astype(jnp.float32),
        lax.psum(shares[11].astype(jnp.bfloat16), ("seq", "ctx")).astype(jnp.float32),
        lax.psum(shares[12].astype(jnp.bfloat16), ("seq", "ctx")).astype(jnp.float32),
        lax.psum(shares[13].astype(jnp.bfloat16), ("seq", "ctx")).astype(jnp.float32),
        lax.psum(shares[14].astype(jnp.bfloat16), ("seq", "ctx")).astype(jnp.float32),
    )
    return (layer_out, grad_input) + tuple(summed)


def solution(mesh):
    in_specs = (
        P(("seq", "wt"), "ctx", None),
        P(("seq", "wt"), "ctx", None),
        P(("seq", "wt"), "ctx"),
        P(("seq", "wt"), None),
        P("wt", None),
        P("wt"),
        P("wt", None),
        P("wt", None),
        P("wt"),
        P("wt", None),
        P("wt"),
        P("wt"),
        P("wt"),
        P("wt", None),
        P("wt"),
        P("wt", None),
        P("wt"),
        P("wt"),
        P("wt"),
    )
    out_specs = (
        P(("seq", "wt"), "ctx", None),
        P(("seq", "wt"), "ctx", None),
        P("wt", None),
        P("wt"),
        P("wt", None),
        P("wt", None),
        P("wt"),
        P("wt", None),
        P("wt"),
        P("wt"),
        P("wt"),
        P("wt", None),
        P("wt"),
        P("wt", None),
        P("wt"),
        P("wt"),
        P("wt"),
    )
    return jax.shard_map(body, mesh=mesh, in_specs=in_specs, out_specs=out_specs, check_vma=False)
```

profile of v0, /device:TPU:0, one launch (start us, length us, event | category | flops | bytes accessed | tf_op | source)
XLA Modules:
  0.0 968.8 jit_solution(11220610871833606484)
XLA Ops:
  17.3 21.1 %all-reduce.20 = (bf16[768]{0:T(1024)(128)(2,1)S(1)}, bf16[768]{0:T(1024)(128)(2,1)S(1)}, bf16[768]{0:T(1024)(128)(2,1)S(1)}, bf16[768]{0:T(1024)(128)(2,1)S(1)}...) all-reduce(bf16[768]{0:T(1024)(128)(2,1)S(1)} %dynamic-update-slice, ...), channel_id=1, replica_groups=mesh['seq'=2,'ctx'=4,'wt'=4] {'wt'}, use_global_device_ids=true, to_apply=%add | all-reduce | flops 5376 | bytes 21504
  38.4 4.9 all-gather.16.cloned.1.call-done
  46.9 27.5 %all-gather.12.cloned.1.call-done = bf16[768,768]{1,0:T(8,128)(2,1)} async-done(((bf16[192,768]{1,0:T(8,128)(2,1)}), bf16[768,768]{1,0:T(8,128)(2,1)}) %all-gather.12.cloned.1.call-update) | async-done | bytes 1179664 | tf_op jit(solution)/shard_map/all_gather | solution.py:114
  81.1 13.6 %all-gather = bf16[4,1,768]{2,1,0:T(2,128)(2,1)S(1)} all-gather(bf16[1,1,768]{2,1,0:T(2,128)(2,1)S(1)} %reshape.309), channel_id=1, replica_groups=mesh['seq'=2,'ctx'=4,'wt'=4] {'wt'}, dimensions={0}, use_global_device_ids=true | all-gather | bytes 7680 | tf_op jit(solution)/shard_map/all_gather | solution.py:122
  94.7 11.1 %all-gather.10.cloned.1.call-done = bf16[768,768]{1,0:T(8,128)(2,1)} async-done(((bf16[192,768]{1,0:T(8,128)(2,1)}), bf16[768,768]{1,0:T(8,128)(2,1)}) %all-gather.10.cloned.1.call-update) | async-done | bytes 1179664 | tf_op jit(solution)/shard_map/all_gather | solution.py:112
  108.5 27.4 %all-gather.18.cloned.1.call-done = bf16[2,1024,768]{1,2,0:T(8,128)(2,1)} async-done(((bf16[2,256,768]{1,2,0:T(8,128)(2,1)}), bf16[2,1024,768]{1,2,0:T(8,128)(2,1)}) %all-gather.18.cloned.1.call-update) | async-done | bytes 3145744 | tf_op jit(solution)/shard_map/all_gather | solution.py:138
  135.8 30.9 %all-gather.14.cloned.1.call-done = bf16[2,1024,768]{1,2,0:T(8,128)(2,1)} async-done(((bf16[2,256,768]{1,2,0:T(8,128)(2,1)}), bf16[2,1024,768]{1,2,0:T(8,128)(2,1)}) %all-gather.14.cloned.1.call-update) | async-done | bytes 3145744 | tf_op jit(solution)/shard_map/all_gather | solution.py:137
  166.9 34.3 %while.26 = (s32[]{:T(128)}, bf16[6,4,256,64]{2,3,1,0:T(8,128)(2,1)S(1)}, f32[6,4,256]{2,1,0:T(4,128)S(1)}, s32[6,256]{1,0:T(8,128)S(1)}, s32[6,1024]{1,0:T(8,12...) while((s32[]{:T(128)}, ...), condition=%wide.region_5.6_spmd, body=%wide.region_2.5_spmd.sunk | while | flops 280230912 | bytes 15123561 | solution.py:157
  205.2 83.6 %all-gather.22.cloned.1.call-done = bf16[768,3072]{1,0:T(8,128)(2,1)} async-done(((bf16[192,3072]{1,0:T(8,128)(2,1)}), bf16[768,3072]{1,0:T(8,128)(2,1)}) %all-gather.22.cloned.1.call-update) | async-done | bytes 4718608 | tf_op jit(solution)/shard_map/all_gather | solution.py:121
  288.8 19.8 %multiply_convert_fusion.1 = (bf16[512,3072]{1,0:T(8,128)(2,1)}, f32[512,3072]{1,0:T(8,128)}, f32[512,3072]{1,0:T(8,128)}) fusion(f32[3072]{0:T(1024)S(1)} %bitcast.251, bf16[768,3072]{1,0:T(8,128)(2,1)} %all-gather.22.cloned.1.call-done, f32[512,768]{1,0:T(8,128)S(1)} %get-tuple-element.307, f32[768]{0:T(1024)S(1)} %convert_element_type.289, ...), kind=kOutput, calls=%fused_computation.68 | convolution fusion | flops 2521694208 | bytes 22042624 | tf_op jit(solution)/shard_map/dot_general | solution.py:14
  308.6 69.7 %all-gather.24.cloned.1.call-done = bf16[3072,768]{1,0:T(8,128)(2,1)} async-done(((bf16[768,768]{1,0:T(8,128)(2,1)}), bf16[3072,768]{1,0:T(8,128)(2,1)}) %all-gather.24.cloned.1.call-update) | async-done | bytes 4718608 | tf_op jit(solution)/shard_map/all_gather | solution.py:123
  378.3 6.1 fusion.78
  388.1 7.9 fusion.71
  396.1 3.1 multiply_reduce_fusion.3
  412.5 83.7 %while.27 = (s32[]{:T(128)}, bf16[6,4,256,64]{2,3,1,0:T(8,128)(2,1)}, bf16[6,4,1024,64]{2,3,1,0:T(8,128)(2,1)}, bf16[6,4,1024,64]{2,3,1,0:T(8,128)(2,1)}, s32[6,...) while((s32[]{:T(128)}, ...), condition=%wide.region_16.17_spmd, body=%wide.region_14.16_spmd.sunk | while | flops 687406080 | bytes 37011584 | solution.py:235
  504.4 28.4 %reduce-scatter.17.cloned.1.call-done = bf16[2,256,768]{1,2,0:T(8,128)(2,1)} async-done(((bf16[2,1024,768]{1,2,0:T(8,128)(2,1)}), bf16[2,256,768]{1,2,0:T(8,128)(2,1)}) %reduce-scatter.17.cloned.1.call-update) | async-done | bytes 786448 | tf_op jit(solution)/shard_map/reduce_scatter | solution.py:244
  532.8 3.2 fusion.62
  538.4 34.9 %reduce-scatter.15.cloned.1.call-done = bf16[2,256,768]{1,2,0:T(8,128)(2,1)} async-done(((bf16[2,1024,768]{1,2,0:T(8,128)(2,1)}), bf16[2,256,768]{1,2,0:T(8,128)(2,1)}) %reduce-scatter.15.cloned.1.call-update) | async-done | bytes 786448 | tf_op jit(solution)/shard_map/reduce_scatter | solution.py:241
  573.3 3.2 fusion.61
  578.9 3.2 convolution_convert_fusion.2
  582.3 7.4 convolution_convert_fusion.1
  589.7 6.9 convolution_convert_fusion
  598.3 6.5 reduce-scatter.25.cloned.1.call-done
  606.7 28.2 %reduce-scatter.29.cloned.1.call-done = bf16[192,768]{1,0:T(8,128)(2,1)} async-done(((bf16[768,768]{1,0:T(8,128)(2,1)}), bf16[192,768]{1,0:T(8,128)(2,1)}) %reduce-scatter.29.cloned.1.call-update) | async-done | bytes 294928
  636.8 28.4 %reduce-scatter.27.cloned.1.call-done = bf16[192,768]{1,0:T(8,128)(2,1)} async-done(((bf16[768,768]{1,0:T(8,128)(2,1)}), bf16[192,768]{1,0:T(8,128)(2,1)}) %reduce-scatter.27.cloned.1.call-update) | async-done | bytes 294928
  667.0 28.8 %reduce-scatter.19.cloned.1.call-done = bf16[192,768]{1,0:T(8,128)(2,1)} async-done(((bf16[768,768]{1,0:T(8,128)(2,1)}), bf16[192,768]{1,0:T(8,128)(2,1)}) %reduce-scatter.19.cloned.1.call-update) | async-done | bytes 294928 | tf_op jit(solution)/shard_map/reduce_scatter | solution.py:292
  695.8 86.2 %reduce-scatter.21.cloned.1.call-done = bf16[192,3072]{1,0:T(8,128)(2,1)} async-done(((bf16[768,3072]{1,0:T(8,128)(2,1)}), bf16[192,3072]{1,0:T(8,128)(2,1)}) %reduce-scatter.21.cloned.1.call-update) | async-done | bytes 1179664 | tf_op jit(solution)/shard_map/reduce_scatter | solution.py:304
  782.0 88.0 %reduce-scatter.23.cloned.1.call-done = bf16[768,768]{1,0:T(8,128)(2,1)} async-done(((bf16[3072,768]{1,0:T(8,128)(2,1)}), bf16[768,768]{1,0:T(8,128)(2,1)}) %reduce-scatter.23.cloned.1.call-update) | async-done | bytes 1179664 | tf_op jit(solution)/shard_map/reduce_scatter | solution.py:310
  874.5 3.5 fusion.79
  879.3 18.2 %all-reduce.19 = (bf16[768]{0:T(1024)(128)(2,1)S(1)}, bf16[768]{0:T(1024)(128)(2,1)S(1)}, bf16[768]{0:T(1024)(128)(2,1)S(1)}, bf16[768]{0:T(1024)(128)(2,1)S(1)}...) all-reduce(bf16[768]{0:T(1024)(128)(2,1)S(1)} %dynamic-update-slice, ...), channel_id=1, replica_groups=mesh['seq'=2,'ctx'=4,'wt'=4] {'wt'}, use_global_device_ids=true, to_apply=%add.7 | all-reduce | flops 9984 | bytes 39936
  898.2 12.5 %all-reduce.17 = (bf16[192]{0:T(256)(128)(2,1)S(1)}, bf16[192]{0:T(256)(128)(2,1)S(1)}, bf16[192]{0:T(256)(128)(2,1)S(1)}, bf16[192]{0:T(256)(128)(2,1)S(1)}, bf...) all-reduce(bf16[192]{0:T(256)(128)(2,1)S(1)} %dynamic-slice.9, ...), channel_id=1, replica_groups=mesh['seq'=2,'ctx'=4,'wt'=4] {'seq','ctx'}, use_global_device_ids=true, to_apply=%region_23.24 | all-reduce | flops 2304 | bytes 9216 | tf_op jit(solution)/shard_map/psum | solution.py:325
  926.0 27.6 %all-reduce.23.cloned.1.call-done = (bf16[192,768]{0,1:T(8,128)(2,1)}, bf16[192,768]{0,1:T(8,128)(2,1)}, bf16[192,768]{0,1:T(8,128)(2,1)}, bf16[192,768]{1,0:T(8...) async-done(((bf16[192,768]{0,1:T(8,128)(2,1)}, bf16[192,768]{0,1:T(8,128)(2,1)}, bf16[192,768]{0,1:T(8,128)(2,1)}, bf16[192,768]{1,0:T(8,128)(2,1)}, ...) | async-done | bytes 3538960 | tf_op jit(solution)/shard_map/psum | solution.py:324
  (306 shorter events, 209.6 us)
Async XLA Ops:
  7.2 36.1 %all-gather.16.cloned.1.call-start = ((), (), s32[]{:S(2)}) async-start(), calls=%async_computation.11 | async-start | bytes 1474560 | tf_op jit(solution)/shard_map/all_gather | solution.py:115
  7.9 66.5 %all-gather.12.cloned.1.call-start = ((), (), s32[]{:S(2)}) async-start(), calls=%async_computation.9 | async-start | bytes 1474560 | tf_op jit(solution)/shard_map/all_gather | solution.py:114
  8.7 97.1 %all-gather.10.cloned.1.call-start = ((), (), s32[]{:S(2)}) async-start(), calls=%async_computation.8 | async-start | bytes 1474560 | tf_op jit(solution)/shard_map/all_gather | solution.py:112
  9.4 126.4 %all-gather.18.cloned.1.call-start = ((), (), s32[]{:S(2)}) async-start(), calls=%async_computation.12 | async-start | bytes 3932160 | tf_op jit(solution)/shard_map/all_gather | solution.py:138
  43.3 31.1 %copy-start.21 = (bf16[2,256,768]{2,1,0:T(8,128)(2,1)S(1)}, bf16[2,256,768]{2,1,0:T(8,128)(2,1)}, u32[]{:S(2)}) copy-start(bf16[2,256,768]{2,1,0:T(8,128)(2,1)} %param.23) | copy-start | bytes 2359300
  46.9 119.9 %all-gather.14.cloned.1.call-start = ((), (), s32[]{:S(2)}) async-start(), calls=%async_computation.10 | async-start | bytes 3932160 | tf_op jit(solution)/shard_map/all_gather | solution.py:137
  76.5 3.9 copy-start.16
  76.5 4.6 copy-start.17
  77.7 124.5 %all-gather.20.cloned.1.call-start = ((), (), s32[]{:S(2)}) async-start(), calls=%async_computation.13 | async-start | bytes 1474560 | tf_op jit(solution)/shard_map/all_gather | solution.py:117
  78.3 210.5 %all-gather.22.cloned.1.call-start = ((), (), s32[]{:S(2)}) async-start(), calls=%async_computation.14 | async-start | bytes 5898240 | tf_op jit(solution)/shard_map/all_gather | solution.py:121
  79.1 299.3 %all-gather.24.cloned.1.call-start = ((), (), s32[]{:S(2)}) async-start(), calls=%async_computation.15 | async-start | bytes 5898240 | tf_op jit(solution)/shard_map/all_gather | solution.py:123
  79.8 453.0 %reduce-scatter.17.cloned.1.call-start = ((), (), s32[]{:S(2)}) async-start(), calls=%async_computation.17 | async-start | bytes 3932160 | tf_op jit(solution)/shard_map/reduce_scatter | solution.py:244
  204.9 191.1 %copy-start.2 = (f32[512,768]{1,0:T(8,128)}, f32[512,768]{1,0:T(8,128)S(1)}, u32[]{:S(2)}) copy-start(f32[512,768]{1,0:T(8,128)S(1)} %get-tuple-element.307) | copy-start | bytes 4718596
  378.3 6.4 copy-start.1
  386.2 9.8 %slice-start = ((s8[4718592]{0:T(1024)(128)(4,1)}), s8[4194304]{0:T(1024)(128)(4,1)S(1)}, s32[]{:S(2)}) async-start(s8[4718592]{0:T(1024)(128)(4,1)} %bitcast.253), calls=%async_computation.25 | async-start | bytes 8388608
  386.4 9.6 copy-start.9
  388.1 8.0 slice-start.1
  496.2 77.0 %reduce-scatter.15.cloned.1.call-start = ((), (), s32[]{:S(2)}) async-start(), calls=%async_computation.16 | async-start | bytes 3932160 | tf_op jit(solution)/shard_map/reduce_scatter | solution.py:241
  496.8 108.0 %reduce-scatter.25.cloned.1.call-start = ((), (), s32[]{:S(2)}) async-start(), calls=%async_computation.21 | async-start | bytes 1474560
  504.3 130.6 %reduce-scatter.29.cloned.1.call-start = ((), (), s32[]{:S(2)}) async-start(), calls=%async_computation.23 | async-start | bytes 1474560
  538.3 126.8 %reduce-scatter.27.cloned.1.call-start = ((), (), s32[]{:S(2)}) async-start(), calls=%async_computation.22 | async-start | bytes 1474560
  578.8 117.0 %reduce-scatter.19.cloned.1.call-start = ((), (), s32[]{:S(2)}) async-start(), calls=%async_computation.18 | async-start | bytes 1474560 | tf_op jit(solution)/shard_map/reduce_scatter | solution.py:292
  582.1 199.9 %reduce-scatter.21.cloned.1.call-start = ((), (), s32[]{:S(2)}) async-start(), calls=%async_computation.19 | async-start | bytes 5898240 | tf_op jit(solution)/shard_map/reduce_scatter | solution.py:304
  589.7 280.3 %reduce-scatter.23.cloned.1.call-start = ((), (), s32[]{:S(2)}) async-start(), calls=%async_computation.20 | async-start | bytes 5898240 | tf_op jit(solution)/shard_map/reduce_scatter | solution.py:310
  596.7 273.3 %copy-start.15 = (f32[2,256]{1,0:T(2,128)S(1)}, f32[2,256]{1,0:T(2,128)}, u32[]{:S(2)}) copy-start(f32[2,256]{1,0:T(2,128)} %get-tuple-element.302) | copy-start | bytes 6148
  596.7 356.9 %all-reduce.23.cloned.1.call-start = ((), (), s32[]{:S(2)}) async-start(), calls=%async_computation.24 | async-start | bytes 7667712 | tf_op jit(solution)/shard_map/psum | solution.py:324
  920.3 3.9 copy-start.3
  920.3 3.9 copy-start.4
  920.4 3.9 copy-start.6
  953.6 4.7 copy-start.14
  953.6 5.5 copy-start.13
  956.7 4.4 copy-start.11
  (12 other events, 32.0 us)
Sparse Core Ops, SparseCore 0:
  9.6 33.6 all-gather.15
  44.9 29.5 all-gather.11
  76.0 29.7 all-gather.9
  107.8 28.0 all-gather.17
  137.8 28.9 all-gather.13
  168.2 30.4 all-gather.19
  200.3 88.5 all-gather.21
  290.4 87.8 all-gather.23
  496.3 36.3 reduce-scatter.16
  535.3 37.9 reduce-scatter.14
  575.6 29.1 reduce-scatter.24
  607.0 27.8 reduce-scatter.28
  637.2 27.8 reduce-scatter.26
  667.9 27.8 reduce-scatter.18
  698.0 83.9 reduce-scatter.20
  784.1 85.7 reduce-scatter.22
  874.5 79.0 all-reduce.22
where the time goes:
time: 975 us; the launch traced here: 969 us
  waiting for transfers between devices  617 us (63%)
  matrix products  181 us (19%)
  blocking collectives  65.3 us (7%)
  local copies, waits for them, and re-layouts  47.2 us (5%)
  other arithmetic  40.5 us (4%)
  between operations  16.7 us (2%)
    reduce_scatter x1, waiting for transfers between devices, body(): lax.psum_scatter(grads[11].astype(jnp.bfloat16), 'wt', scatter_dimension=...  88 us
    reduce_scatter x1, waiting for transfers between devices, body(): lax.psum_scatter(grads[9].astype(jnp.bfloat16), 'wt', scatter_dimension=0...  86.2 us
    all_gather x1, waiting for transfers between devices, body(): lax.all_gather(shards[9], 'wt', axis=0, tiled=True)  83.6 us
    all_gather x1, waiting for transfers between devices, body(): lax.all_gather(shards[11], 'wt', axis=0, tiled=True)  69.7 us
    unnamed x20, waiting for transfers between devices  67.8 us
    unnamed x2, blocking collectives  39.3 us
    dot_general x6, matrix products, product(): return jnp.dot(former, latter, preferred_element_type=jnp.float32)  35 us
    reduce_scatter x1, waiting for transfers between devices, body(): lax.psum_scatter(partial_kv[0].astype(jnp.bfloat16), 'ctx', scatter_dimen...  34.9 us
  transfers between devices with their start and end apart: 17, of which 16 were waited for; matrix products, arithmetic and copies ran while one was open for 15% of the time, Pallas kernels for 0%

commit v1 on v0

--- a/solution.py
+++ b/solution.py
@@ -321,7 +321,7 @@
         ).astype(jnp.float32),
     )
     summed = (
-        lax.psum(shares[0].astype(jnp.bfloat16), ("seq", "ctx")).astype(jnp.float32),
+        lax.psum(lax.psum(shares[0].astype(jnp.bfloat16), "ctx"), "seq").astype(jnp.float32),
         lax.psum(shares[1].astype(jnp.bfloat16), ("seq", "ctx")).astype(jnp.float32),
         lax.psum(shares[2].astype(jnp.bfloat16), ("seq", "ctx")).astype(jnp.float32),
         lax.psum(shares[3].astype(jnp.bfloat16), ("seq", "ctx")).astype(jnp.float32),

time: 975 us -> 1040 us (1.067)
  waiting for transfers between devices: 617 us -> 681 us
    psum x1 -> x3, waiting for transfers between devices: 27.6 us -> 58.9 us  [the longest x1 28 us: body(): lax.psum(shares[2].astype(jnp.bfloat16), ('seq', 'ctx')).astype(jnp.float32)]
    unnamed x20 -> x22, waiting for transfers between devices: 67.8 us -> 91.7 us
    unnamed x93 -> x91, local copies, waits for them, and re-layouts: 27.9 us -> 28.7 us
  transfers between devices with their start and end apart: 17 -> 19, of which waited for: 16 -> 18; matrix products, arithmetic and copies ran while one was open for 15% -> 13% of each run, Pallas kernels for 0% -> 0%
where the time goes in v1:
time: 1040 us; the launch traced here: 1030 us
  waiting for transfers between devices  681 us (65%)
  matrix products  181 us (17%)
  blocking collectives  66 us (6%)
  local copies, waits for them, and re-layouts  48 us (5%)
  other arithmetic  40.5 us (4%)
  between operations  16.8 us (2%)
    unnamed x22, waiting for transfers between devices  91.7 us
    reduce_scatter x1, waiting for transfers between devices, body(): lax.psum_scatter(grads[11].astype(jnp.bfloat16), 'wt', scatter_dimension=...  88.1 us
    reduce_scatter x1, waiting for transfers between devices, body(): lax.psum_scatter(grads[9].astype(jnp.bfloat16), 'wt', scatter_dimension=0...  86.3 us
    all_gather x1, waiting for transfers between devices, body(): lax.all_gather(shards[9], 'wt', axis=0, tiled=True)  83.6 us
    all_gather x1, waiting for transfers between devices, body(): lax.all_gather(shards[11], 'wt', axis=0, tiled=True)  69.7 us
    unnamed x2, blocking collectives  40 us
    reduce_scatter x1, waiting for transfers between devices, body(): lax.psum_scatter(partial_kv[1].astype(jnp.bfloat16), 'ctx', scatter_dimen...  37.1 us
    reduce_scatter x1, waiting for transfers between devices, body(): lax.psum_scatter(partial_kv[0].astype(jnp.bfloat16), 'ctx', scatter_dimen...  35.1 us
  transfers between devices with their start and end apart: 19, of which 18 were waited for; matrix products, arithmetic and copies ran while one was open for 13% of the time, Pallas kernels for 0%

profile of v1, /device:TPU:0, one launch (start us, length us, event | category | flops | bytes accessed | tf_op | source)
XLA Modules:
  0.0 1034.9 jit_solution(3702302328689434122)
XLA Ops:
  17.3 21.1 %all-reduce.20 = (bf16[768]{0:T(1024)(128)(2,1)S(1)}, bf16[768]{0:T(1024)(128)(2,1)S(1)}, bf16[768]{0:T(1024)(128)(2,1)S(1)}, bf16[768]{0:T(1024)(128)(2,1)S(1)}...) all-reduce(bf16[768]{0:T(1024)(128)(2,1)S(1)} %dynamic-update-slice, ...), channel_id=1, replica_groups=mesh['seq'=2,'ctx'=4,'wt'=4] {'wt'}, use_global_device_ids=true, to_apply=%add | all-reduce | flops 5376 | bytes 21504
  38.4 4.9 all-gather.16.cloned.1.call-done
  46.9 27.5 %all-gather.12.cloned.1.call-done = bf16[768,768]{1,0:T(8,128)(2,1)} async-done(((bf16[192,768]{1,0:T(8,128)(2,1)}), bf16[768,768]{1,0:T(8,128)(2,1)}) %all-gather.12.cloned.1.call-update) | async-done | bytes 1179664 | tf_op jit(solution)/shard_map/all_gather | solution.py:114
  81.1 13.6 %all-gather = bf16[4,1,768]{2,1,0:T(2,128)(2,1)S(1)} all-gather(bf16[1,1,768]{2,1,0:T(2,128)(2,1)S(1)} %reshape.309), channel_id=1, replica_groups=mesh['seq'=2,'ctx'=4,'wt'=4] {'wt'}, dimensions={0}, use_global_device_ids=true | all-gather | bytes 7680 | tf_op jit(solution)/shard_map/all_gather | solution.py:122
  94.7 11.1 %all-gather.10.cloned.1.call-done = bf16[768,768]{1,0:T(8,128)(2,1)} async-done(((bf16[192,768]{1,0:T(8,128)(2,1)}), bf16[768,768]{1,0:T(8,128)(2,1)}) %all-gather.10.cloned.1.call-update) | async-done | bytes 1179664 | tf_op jit(solution)/shard_map/all_gather | solution.py:112
  108.5 27.4 %all-gather.18.cloned.1.call-done = bf16[2,1024,768]{1,2,0:T(8,128)(2,1)} async-done(((bf16[2,256,768]{1,2,0:T(8,128)(2,1)}), bf16[2,1024,768]{1,2,0:T(8,128)(2,1)}) %all-gather.18.cloned.1.call-update) | async-done | bytes 3145744 | tf_op jit(solution)/shard_map/all_gather | solution.py:138
  135.8 30.9 %all-gather.14.cloned.1.call-done = bf16[2,1024,768]{1,2,0:T(8,128)(2,1)} async-done(((bf16[2,256,768]{1,2,0:T(8,128)(2,1)}), bf16[2,1024,768]{1,2,0:T(8,128)(2,1)}) %all-gather.14.cloned.1.call-update) | async-done | bytes 3145744 | tf_op jit(solution)/shard_map/all_gather | solution.py:137
  166.9 34.3 %while.26 = (s32[]{:T(128)}, bf16[6,4,256,64]{2,3,1,0:T(8,128)(2,1)S(1)}, f32[6,4,256]{2,1,0:T(4,128)S(1)}, s32[6,256]{1,0:T(8,128)S(1)}, s32[6,1024]{1,0:T(8,12...) while((s32[]{:T(128)}, ...), condition=%wide.region_5.6_spmd, body=%wide.region_2.5_spmd.sunk | while | flops 280230912 | bytes 15123561 | solution.py:157
  205.2 83.6 %all-gather.22.cloned.1.call-done = bf16[768,3072]{1,0:T(8,128)(2,1)} async-done(((bf16[192,3072]{1,0:T(8,128)(2,1)}), bf16[768,3072]{1,0:T(8,128)(2,1)}) %all-gather.22.cloned.1.call-update) | async-done | bytes 4718608 | tf_op jit(solution)/shard_map/all_gather | solution.py:121
  288.8 19.8 %multiply_convert_fusion.1 = (bf16[512,3072]{1,0:T(8,128)(2,1)}, f32[512,3072]{1,0:T(8,128)}, f32[512,3072]{1,0:T(8,128)}) fusion(f32[3072]{0:T(1024)S(1)} %bitcast.251, bf16[768,3072]{1,0:T(8,128)(2,1)} %all-gather.22.cloned.1.call-done, f32[512,768]{1,0:T(8,128)S(1)} %get-tuple-element.306, f32[768]{0:T(1024)S(1)} %convert_element_type.289, ...), kind=kOutput, calls=%fused_computation.68 | convolution fusion | flops 2521694208 | bytes 22042624 | tf_op jit(solution)/shard_map/dot_general | solution.py:14
  308.6 69.7 %all-gather.24.cloned.1.call-done = bf16[3072,768]{1,0:T(8,128)(2,1)} async-done(((bf16[768,768]{1,0:T(8,128)(2,1)}), bf16[3072,768]{1,0:T(8,128)(2,1)}) %all-gather.24.cloned.1.call-update) | async-done | bytes 4718608 | tf_op jit(solution)/shard_map/all_gather | solution.py:123
  378.3 6.1 fusion.78
  388.1 7.9 fusion.71
  412.5 83.7 %while.27 = (s32[]{:T(128)}, bf16[6,4,256,64]{2,3,1,0:T(8,128)(2,1)}, bf16[6,4,1024,64]{2,3,1,0:T(8,128)(2,1)}, bf16[6,4,1024,64]{2,3,1,0:T(8,128)(2,1)}, s32[6,...) while((s32[]{:T(128)}, ...), condition=%wide.region_16.17_spmd, body=%wide.region_14.16_spmd.sunk | while | flops 687406080 | bytes 37011584 | solution.py:235
  504.8 26.4 %reduce-scatter.25.cloned.1.call-done = bf16[192,768]{1,0:T(8,128)(2,1)} async-done(((bf16[768,768]{1,0:T(8,128)(2,1)}), bf16[192,768]{1,0:T(8,128)(2,1)}) %reduce-scatter.25.cloned.1.call-update) | async-done | bytes 294928
  533.2 37.1 %reduce-scatter.17.cloned.1.call-done = bf16[2,256,768]{1,2,0:T(8,128)(2,1)} async-done(((bf16[2,1024,768]{1,2,0:T(8,128)(2,1)}), bf16[2,256,768]{1,2,0:T(8,128)(2,1)}) %reduce-scatter.17.cloned.1.call-update) | async-done | bytes 786448 | tf_op jit(solution)/shard_map/reduce_scatter | solution.py:244
  570.3 3.2 fusion.62
  575.9 35.1 %reduce-scatter.15.cloned.1.call-done = bf16[2,256,768]{1,2,0:T(8,128)(2,1)} async-done(((bf16[2,1024,768]{1,2,0:T(8,128)(2,1)}), bf16[2,256,768]{1,2,0:T(8,128)(2,1)}) %reduce-scatter.15.cloned.1.call-update) | async-done | bytes 786448 | tf_op jit(solution)/shard_map/reduce_scatter | solution.py:241
  616.6 3.2 convolution_convert_fusion.2
  620.0 7.4 convolution_convert_fusion.1
  627.4 6.9 convolution_convert_fusion
  634.5 11.9 %all-reduce.25.cloned.1.call-done = bf16[192,768]{0,1:T(8,128)(2,1)} async-done(((bf16[192,768]{0,1:T(8,128)(2,1)}), bf16[192,768]{0,1:T(8,128)(2,1)}) %all-reduce.25.cloned.1.call-update) | async-done | bytes 294928 | tf_op jit(solution)/shard_map/psum | solution.py:324
  646.5 31.6 %reduce-scatter.29.cloned.1.call-done = bf16[192,768]{1,0:T(8,128)(2,1)} async-done(((bf16[768,768]{1,0:T(8,128)(2,1)}), bf16[192,768]{1,0:T(8,128)(2,1)}) %reduce-scatter.29.cloned.1.call-update) | async-done | bytes 294928
  679.9 28.3 %reduce-scatter.27.cloned.1.call-done = bf16[192,768]{1,0:T(8,128)(2,1)} async-done(((bf16[768,768]{1,0:T(8,128)(2,1)}), bf16[192,768]{1,0:T(8,128)(2,1)}) %reduce-scatter.27.cloned.1.call-update) | async-done | bytes 294928
  710.1 28.9 %reduce-scatter.19.cloned.1.call-done = bf16[192,768]{1,0:T(8,128)(2,1)} async-done(((bf16[768,768]{1,0:T(8,128)(2,1)}), bf16[192,768]{1,0:T(8,128)(2,1)}) %reduce-scatter.19.cloned.1.call-update) | async-done | bytes 294928 | tf_op jit(solution)/shard_map/reduce_scatter | solution.py:292
  739.0 86.3 %reduce-scatter.21.cloned.1.call-done = bf16[192,3072]{1,0:T(8,128)(2,1)} async-done(((bf16[768,3072]{1,0:T(8,128)(2,1)}), bf16[192,3072]{1,0:T(8,128)(2,1)}) %reduce-scatter.21.cloned.1.call-update) | async-done | bytes 1179664 | tf_op jit(solution)/shard_map/reduce_scatter | solution.py:304
  825.3 88.1 %reduce-scatter.23.cloned.1.call-done = bf16[768,768]{1,0:T(8,128)(2,1)} async-done(((bf16[3072,768]{1,0:T(8,128)(2,1)}), bf16[768,768]{1,0:T(8,128)(2,1)}) %reduce-scatter.23.cloned.1.call-update) | async-done | bytes 1179664 | tf_op jit(solution)/shard_map/reduce_scatter | solution.py:310
  919.4 3.5 fusion.79
  922.9 18.9 %all-reduce.27.cloned.1.call-done = bf16[192,768]{0,1:T(8,128)(2,1)} async-done(((bf16[192,768]{0,1:T(8,128)(2,1)}), bf16[192,768]{0,1:T(8,128)(2,1)}) %all-reduce.27.cloned.1.call-update) | async-done | bytes 294928 | tf_op jit(solution)/shard_map/psum | solution.py:324
  945.2 19.0 %all-reduce.19 = (bf16[768]{0:T(1024)(128)(2,1)S(1)}, bf16[768]{0:T(1024)(128)(2,1)S(1)}, bf16[768]{0:T(1024)(128)(2,1)S(1)}, bf16[768]{0:T(1024)(128)(2,1)S(1)}...) all-reduce(bf16[768]{0:T(1024)(128)(2,1)S(1)} %dynamic-update-slice, ...), channel_id=1, replica_groups=mesh['seq'=2,'ctx'=4,'wt'=4] {'wt'}, use_global_device_ids=true, to_apply=%add.7 | all-reduce | flops 9984 | bytes 39936
  964.8 12.4 %all-reduce.17 = (bf16[192]{0:T(256)(128)(2,1)S(1)}, bf16[192]{0:T(256)(128)(2,1)S(1)}, bf16[192]{0:T(256)(128)(2,1)S(1)}, bf16[192]{0:T(256)(128)(2,1)S(1)}, bf...) all-reduce(bf16[192]{0:T(256)(128)(2,1)S(1)} %dynamic-slice.9, ...), channel_id=1, replica_groups=mesh['seq'=2,'ctx'=4,'wt'=4] {'seq','ctx'}, use_global_device_ids=true, to_apply=%region_24.25 | all-reduce | flops 2304 | bytes 9216 | tf_op jit(solution)/shard_map/psum | solution.py:325
  992.6 28.0 %all-reduce.29.cloned.1.call-done = (bf16[192,768]{0,1:T(8,128)(2,1)}, bf16[192,768]{0,1:T(8,128)(2,1)}, bf16[192,768]{1,0:T(8,128)(2,1)}, bf16[192,3072]{1,0:T(8,128)(2,1)}, bf16[768,768]{1,0:T(8,128)(2,1)}) async-done(((bf16[192,768]{0,1:T(8,128)(2,1)}, bf16[192,768]{0,1:T(8,128)(2,1)}, bf16[192,768]{1,0:T(8,128)(2,1)}, bf16[192,3072]{1,0:T(8,128)(2,1)}, bf16[768,768]{1,0:T(8,128)(2,1)}), ...) | async-done | bytes 3244048 | tf_op jit(solution)/shard_map/psum | solution.py:326
  (310 shorter events, 217.5 us)
Async XLA Ops:
  7.2 36.1 %all-gather.16.cloned.1.call-start = ((), (), s32[]{:S(2)}) async-start(), calls=%async_computation.11 | async-start | bytes 1474560 | tf_op jit(solution)/shard_map/all_gather | solution.py:115
  7.9 66.5 %all-gather.12.cloned.1.call-start = ((), (), s32[]{:S(2)}) async-start(), calls=%async_computation.9 | async-start | bytes 1474560 | tf_op jit(solution)/shard_map/all_gather | solution.py:114
  8.7 97.1 %all-gather.10.cloned.1.call-start = ((), (), s32[]{:S(2)}) async-start(), calls=%async_computation.8 | async-start | bytes 1474560 | tf_op jit(solution)/shard_map/all_gather | solution.py:112
  9.4 126.4 %all-gather.18.cloned.1.call-start = ((), (), s32[]{:S(2)}) async-start(), calls=%async_computation.12 | async-start | bytes 3932160 | tf_op jit(solution)/shard_map/all_gather | solution.py:138
  43.3 31.1 %copy-start.20 = (bf16[2,256,768]{2,1,0:T(8,128)(2,1)S(1)}, bf16[2,256,768]{2,1,0:T(8,128)(2,1)}, u32[]{:S(2)}) copy-start(bf16[2,256,768]{2,1,0:T(8,128)(2,1)} %param.23) | copy-start | bytes 2359300
  46.9 119.9 %all-gather.14.cloned.1.call-start = ((), (), s32[]{:S(2)}) async-start(), calls=%async_computation.10 | async-start | bytes 3932160 | tf_op jit(solution)/shard_map/all_gather | solution.py:137
  76.5 3.9 copy-start.15
  76.5 4.6 copy-start.16
  77.7 124.5 %all-gather.20.cloned.1.call-start = ((), (), s32[]{:S(2)}) async-start(), calls=%async_computation.13 | async-start | bytes 1474560 | tf_op jit(solution)/shard_map/all_gather | solution.py:117
  78.3 210.5 %all-gather.22.cloned.1.call-start = ((), (), s32[]{:S(2)}) async-start(), calls=%async_computation.14 | async-start | bytes 5898240 | tf_op jit(solution)/shard_map/all_gather | solution.py:121
  79.1 299.3 %all-gather.24.cloned.1.call-start = ((), (), s32[]{:S(2)}) async-start(), calls=%async_computation.15 | async-start | bytes 5898240 | tf_op jit(solution)/shard_map/all_gather | solution.py:123
  79.8 451.4 %reduce-scatter.25.cloned.1.call-start = ((), (), s32[]{:S(2)}) async-start(), calls=%async_computation.23 | async-start | bytes 1474560
  204.9 191.1 %copy-start.2 = (f32[512,768]{1,0:T(8,128)}, f32[512,768]{1,0:T(8,128)S(1)}, u32[]{:S(2)}) copy-start(f32[512,768]{1,0:T(8,128)S(1)} %get-tuple-element.306) | copy-start | bytes 4718596
  378.3 6.4 copy-start.1
  386.2 9.8 slice-start
  386.4 9.6 copy-start.9
  388.1 7.9 slice-start.1
  503.4 66.9 %reduce-scatter.17.cloned.1.call-start = ((), (), s32[]{:S(2)}) async-start(), calls=%async_computation.17 | async-start | bytes 3932160 | tf_op jit(solution)/shard_map/reduce_scatter | solution.py:244
  504.0 106.9 %reduce-scatter.15.cloned.1.call-start = ((), (), s32[]{:S(2)}) async-start(), calls=%async_computation.16 | async-start | bytes 3932160 | tf_op jit(solution)/shard_map/reduce_scatter | solution.py:241
  504.8 141.7 %all-reduce.25.cloned.1.call-start = ((), (), s32[]{:S(2)}) async-start(), calls=%async_computation.18 | async-start | bytes 786432 | tf_op jit(solution)/shard_map/psum | solution.py:324
  533.1 144.9 %reduce-scatter.29.cloned.1.call-start = ((), (), s32[]{:S(2)}) async-start(), calls=%async_computation.25 | async-start | bytes 1474560
  575.8 132.4 %reduce-scatter.27.cloned.1.call-start = ((), (), s32[]{:S(2)}) async-start(), calls=%async_computation.24 | async-start | bytes 1474560
  616.5 122.5 %reduce-scatter.19.cloned.1.call-start = ((), (), s32[]{:S(2)}) async-start(), calls=%async_computation.20 | async-start | bytes 1474560 | tf_op jit(solution)/shard_map/reduce_scatter | solution.py:292
  619.8 205.5 %reduce-scatter.21.cloned.1.call-start = ((), (), s32[]{:S(2)}) async-start(), calls=%async_computation.21 | async-start | bytes 5898240 | tf_op jit(solution)/shard_map/reduce_scatter | solution.py:304
  627.4 286.0 %reduce-scatter.23.cloned.1.call-start = ((), (), s32[]{:S(2)}) async-start(), calls=%async_computation.22 | async-start | bytes 5898240 | tf_op jit(solution)/shard_map/reduce_scatter | solution.py:310
  634.4 279.0 %copy-start.14 = (f32[2,256]{1,0:T(2,128)S(1)}, f32[2,256]{1,0:T(2,128)}, u32[]{:S(2)}) copy-start(f32[2,256]{1,0:T(2,128)} %get-tuple-element.301) | copy-start | bytes 6148
  634.4 281.6 %copy-start.22 = (bf16[192]{0:T(256)(128)(2,1)S(1)}, bf16[192]{0:T(256)(128)(2,1)}, u32[]{:S(2)}) copy-start(bf16[192]{0:T(256)(128)(2,1)} %param.41) | copy-start | bytes 1156
  634.4 307.4 %all-reduce.27.cloned.1.call-start = ((), (), s32[]{:S(2)}) async-start(), calls=%async_computation.19 | async-start | bytes 786432 | tf_op jit(solution)/shard_map/psum | solution.py:324
  646.4 374.2 %all-reduce.29.cloned.1.call-start = ((), (), s32[]{:S(2)}) async-start(), calls=%async_computation.26 | async-start | bytes 6881280 | tf_op jit(solution)/shard_map/psum | solution.py:326
  986.9 3.9 copy-start.6
  1020.7 4.7 copy-start.13
  1020.7 5.5 copy-start.12
  (13 other events, 38.3 us)
Sparse Core Ops, SparseCore 0:
  9.6 33.6 all-gather.15
  44.9 29.5 all-gather.11
  76.0 29.7 all-gather.9
  107.8 28.0 all-gather.17
  137.8 28.9 all-gather.13
  168.2 30.4 all-gather.19
  200.3 88.5 all-gather.21
  290.4 87.8 all-gather.23
  503.5 27.6 reduce-scatter.24
  533.6 36.6 reduce-scatter.16
  573.0 37.9 reduce-scatter.14
  613.7 32.6 all-reduce.24
  648.8 29.1 reduce-scatter.28
  680.3 27.8 reduce-scatter.26
  711.1 27.8 reduce-scatter.18
  741.3 83.9 reduce-scatter.20
  827.5 85.7 reduce-scatter.22
  915.6 26.2 all-reduce.26
  946.4 74.1 all-reduce.28
